TPU v7x, 256 devices: a whole 4x4x8 slice. The times are simulated.
256 devices in a mesh: wide: 32 (over z, y), narrow: 8 (over x, core).
Axes of the slice: x: 4, y: 4, z: 8, core: 2. Of those that a mesh axis runs over, the one named last changes fastest.
Arguments:
- flow_panels: float32 [256, 65536], P('wide', 'narrow'), may hold values from 0.01 to 1
- tile_values: float32 [49152, 128, 128], P(('wide', 'narrow'))
- tile_coords: int32 [49152, 2], P(('wide', 'narrow')), may hold values from 0 to 15, as said below
- tile_lists: int32 [32, 128], P(None, 'narrow'), may hold values from 0 to 63, as said below
- keep_masks: int32 [2, 256, 512], P(None, 'wide', 'narrow'), may hold values 0 or 1
Outputs:
- next_flow: float32 [256, 65536], P('wide', 'narrow')
Inputs may be any that keep to these rules, and one draw needn't show every extreme that they name: `tile_coords`: on each device the 192 pairs (row block, list slot) are different; the row block is below 16 and the slot below 16. `tile_lists`: for every pair of a wide index and a narrow index the 16 entries name different vertex blocks among that narrow index's 64.
All inputs are finite; a program needn't handle non-finite values. No bound on the sum of `keep_masks` on one device may be relied on, other than what follows from the above.
Results may differ from a plain program's by a relative error of at most 0.0001.
Values sent between devices are 32-bit elements; how exact they have to be, the bound alone decides.
A program may use at most 128 MiB of HBM per device.

v0:
```python
import jax
import jax.numpy as jnp
from jax import lax
from jax.sharding import PartitionSpec as P

ROW_BLOCKS = 16
ITERS = 2


epsilon = 1e-06


def local(flow_panels, tile_values, tile_coords, tile_lists, keep_masks):
    panel_rows, own_width = flow_panels.shape
    tile_side = tile_values.shape[1]
    col_blocks = own_width // tile_side
    listed = tile_lists.shape[1]
    wide_count = lax.axis_size("wide")
    tile_grid = jnp.zeros((ROW_BLOCKS, listed, tile_side, tile_side), jnp.float32)
    tile_grid = tile_grid.at[tile_coords[:, 0], tile_coords[:, 1]].add(tile_values)
    matrix = tile_grid.transpose(0, 2, 1, 3).reshape(ROW_BLOCKS * tile_side, listed * tile_side)
    own_list = lax.dynamic_index_in_dim(tile_lists, lax.axis_index("wide"), 0, keepdims=False)
    current = flow_panels
    for iteration in range(ITERS):
        slab_rows = lax.all_gather(current, "wide", axis=0, tiled=True)
        row_count = slab_rows.shape[0]
        chosen = jnp.take(slab_rows.reshape(row_count, col_blocks, tile_side), own_list, axis=1)
        chosen = chosen.reshape(row_count, listed * tile_side)
        stacked = lax.dot_general(
            chosen,
            matrix,
            (((1,), (1,)), ((), ())),
            precision=lax.Precision.HIGHEST,
            preferred_element_type=jnp.float32,
        )
        partial_value = stacked.reshape(wide_count, panel_rows, ROW_BLOCKS * tile_side)
        returned = lax.all_to_all(partial_value, "wide", split_axis=0, concat_axis=2, tiled=True)
        totals_in = returned.reshape(returned.shape[1], -1)
        kept = keep_masks[iteration].astype(jnp.float32)
        summed = lax.psum(totals_in, "narrow")
        squared = summed * summed
        col_scale = jnp.mean(squared, axis=1, keepdims=True) + epsilon
        own_rows = lax.dynamic_slice_in_dim(
            squared, lax.axis_index("narrow") * own_width, own_width, 1
        )
        normal = own_rows / col_scale
        current = (normal.reshape(panel_rows, col_blocks, tile_side) * kept[:, :, None]).reshape(
            panel_rows, own_width
        )
    return current


def solution(mesh):
    return jax.shard_map(
        local,
        mesh=mesh,
        in_specs=(
            P("wide", "narrow"),
            P(("wide", "narrow"), None, None),
            P(("wide", "narrow"), None),
            P(None, "narrow"),
            P(None, "wide", "narrow"),
        ),
        out_specs=P("wide", "narrow"),
        check_vma=False,
    )
```

profile of v0, /device:TPU:1, one launch (start us, length us, event | category | flops | bytes accessed | tf_op | source)
XLA Modules:
  0.0 555.9 jit_solution(9310291740815231691)
XLA Ops:
  6.5 0.0 copy-start
  6.5 0.0 all-gather.3.cloned.1.call-start
  6.5 0.7 all-gather.3.cloned.1.call-update
  7.3 0.0 all-reduce.3.cloned.1.call-start
  7.3 0.8 or_select_fusion
  8.1 7.8 %broadcast_in_dim.11 = f32[16,16,128,128]{3,2,1,0:T(8,128)} broadcast(f32[]{:T(128)} %constant.12.clone.1), dimensions={} | broadcast | bytes 16777220 | tf_op jit(solution)/shard_map/broadcast_in_dim | solution.py:19
  15.9 41.5 %scatter_fusion = f32[16,16,128,128]{3,2,1,0:T(8,128)} fusion(f32[16,16,128,128]{3,2,1,0:T(8,128)} %broadcast_in_dim.11, s32[192]{0:T(256)S(1)} %bitcast.35, f32[192,128,128]{2,1,0:T(8,128)} %param.8), kind=kCustom, calls=%fused_computation.2 | custom fusion | flops 3145728 | bytes 37750272 | tf_op jit(solution)/shard_map/scatter-add | solution.py:20
  57.4 17.7 %copy.30 = f32[16,128,16,128]{3,2,1,0:T(8,128)} copy(f32[16,128,16,128]{3,1,2,0:T(8,128)} %bitcast.32) | data formatting | bytes 33554432 | tf_op jit(solution)/shard_map/transpose | solution.py:21
  75.1 18.1 %reshape.93 = f32[2048,2048,1]{1,0,2:T(8,128)} reshape(f32[16,128,16,128]{3,2,1,0:T(8,128)} %copy.30) | data formatting | bytes 33554432 | tf_op jit(solution)/shard_map/reshape | solution.py:21
  93.2 0.0 copy-done
  93.3 0.2 dynamic-slice_reduce_fusion
  93.5 18.3 %all-gather.3.cloned.1.call-done = f32[256,8192]{1,0:T(8,128)} async-done(((f32[8,8192]{1,0:T(8,128)}), f32[256,8192]{1,0:T(8,128)}) %all-gather.3.cloned.1.call-update) | async-done | bytes 8388624 | tf_op jit(solution)/shard_map/all_gather | solution.py:25
  111.8 9.0 %copy.27 = f32[256,8192]{0,1:T(8,128)} copy(f32[256,8192]{1,0:T(8,128)} %all-gather.3.cloned.1.call-done) | data formatting | bytes 16777216 | tf_op jit(solution)/shard_map/all_gather | solution.py:25
  120.7 9.0 %copy.28 = f32[256,64,128]{2,0,1:T(8,128)} copy(f32[256,64,128]{0,2,1:T(8,128)} %bitcast.33) | data formatting | bytes 16777216 | tf_op jit(solution)/shard_map/reshape | solution.py:27
  129.7 4.1 gather_fusion
  133.8 0.3 select_bitcast_fusion.1
  134.1 2.6 copy.29
  136.6 1.7 dot_general.10
  138.3 17.0 %fusion.1 = f32[32,8,2048]{2,1,0:T(8,128)S(1)} fusion(f32[32,8,2048]{2,1,0:T(8,128)S(1)} %dot_general.10, f32[2048,2048,1]{1,0,2:T(8,128)} %reshape.93), kind=kOutput, calls=%fused_computation.23 | convolution fusion | flops 12884901888 | bytes 20971520 | tf_op jit(solution)/shard_map/dot_general | solution.py:29
  155.4 53.5 %all_to_all.30 = f32[32,8,2048]{2,1,0:T(8,128)} all-to-all(f32[32,8,2048]{2,1,0:T(8,128)S(1)} %fusion.1), channel_id=1, replica_groups=mesh['wide'=32,'narrow'=8] {'wide'}, dimensions={0} | all-to-all | bytes 4194304 | tf_op jit(solution)/shard_map/all_to_all | solution.py:37
  208.9 0.0 copy-start.2
  208.9 0.0 all-reduce.3.cloned.1.call-update
  209.0 0.0 all-gather.5.cloned.1.call-start
  209.0 0.6 copy-done.2
  209.6 0.1 copy.31
  209.7 67.8 %all-reduce.3.cloned.1.call-done = f32[8,65536]{1,0:T(8,128)} async-done(((f32[8,65536]{1,0:T(8,128)}), f32[8,65536]{1,0:T(8,128)}) %all-reduce.3.cloned.1.call-update) | async-done | bytes 2097168 | tf_op jit(solution)/shard_map/psum | solution.py:40
  277.5 2.2 multiply_reduce_fusion.1
  279.8 0.8 bitcast_multiply_fusion.1
  280.6 0.0 all-gather.5.cloned.1.call-update
  280.6 0.2 all-reduce.5.cloned.1.call-start
  280.9 99.6 %all-gather.5.cloned.1.call-done = f32[256,8192]{1,0:T(8,128)} async-done(((f32[8,8192]{1,0:T(8,128)}), f32[256,8192]{1,0:T(8,128)}) %all-gather.5.cloned.1.call-update) | async-done | bytes 8388624 | tf_op jit(solution)/shard_map/all_gather | solution.py:25
  380.5 9.0 %copy.32 = f32[256,8192]{0,1:T(8,128)} copy(f32[256,8192]{1,0:T(8,128)} %all-gather.5.cloned.1.call-done) | data formatting | bytes 16777216 | tf_op jit(solution)/shard_map/all_gather | solution.py:25
  389.5 9.0 %copy.33 = f32[256,64,128]{2,0,1:T(8,128)} copy(f32[256,64,128]{0,2,1:T(8,128)} %bitcast.34) | data formatting | bytes 16777216 | tf_op jit(solution)/shard_map/reshape | solution.py:27
  398.4 4.1 gather_fusion.1
  402.5 0.3 select_bitcast_fusion
  402.8 2.6 copy.34
  405.3 1.7 dot_general.12
  407.1 17.1 %fusion.2 = f32[32,8,2048]{2,1,0:T(8,128)S(1)} fusion(f32[32,8,2048]{2,1,0:T(8,128)S(1)} %dot_general.12, f32[2048,2048,1]{1,0,2:T(8,128)} %reshape.93), kind=kOutput, calls=%fused_computation.24 | convolution fusion | flops 12884901888 | bytes 20971520 | tf_op jit(solution)/shard_map/dot_general | solution.py:29
  424.1 53.5 %all_to_all.31 = f32[32,8,2048]{2,1,0:T(8,128)} all-to-all(f32[32,8,2048]{2,1,0:T(8,128)S(1)} %fusion.2), channel_id=1, replica_groups=mesh['wide'=32,'narrow'=8] {'wide'}, dimensions={0} | all-to-all | bytes 4194304 | tf_op jit(solution)/shard_map/all_to_all | solution.py:37
  477.7 0.0 all-reduce.5.cloned.1.call-update
  477.7 0.0 copy-start.1
  477.7 0.1 copy.35
  477.8 68.5 %all-reduce.5.cloned.1.call-done = f32[8,65536]{1,0:T(8,128)} async-done(((f32[8,65536]{1,0:T(8,128)}), f32[8,65536]{1,0:T(8,128)}) %all-reduce.5.cloned.1.call-update) | async-done | bytes 2097168 | tf_op jit(solution)/shard_map/psum | solution.py:40
  546.3 2.2 multiply_reduce_fusion
  548.5 0.8 bitcast_multiply_fusion
  549.4 0.0 copy-done.1
  (6 shorter events, 0.0 us)
Async XLA Ops:
  6.5 86.7 %copy-start = (s32[32,16]{0,1:T(8,128)S(1)}, s32[32,16]{0,1:T(8,128)}, u32[]{:S(2)}) copy-start(s32[32,16]{0,1:T(8,128)} %param.10) | copy-start | bytes 6148
  6.5 105.2 %all-gather.3.cloned.1.call-start = ((), (), s32[]{:S(2)}) async-start(), calls=%async_computation.2 | async-start | bytes 8650752 | tf_op jit(solution)/shard_map/all_gather | solution.py:25
  7.3 270.2 %all-reduce.3.cloned.1.call-start = ((), (), s32[]{:S(2)}) async-start(), calls=%async_computation.3 | async-start | bytes 4194304 | tf_op jit(solution)/shard_map/psum | solution.py:40
  208.9 0.7 copy-start.2
  209.0 171.5 %all-gather.5.cloned.1.call-start = ((), (), s32[]{:S(2)}) async-start(), calls=%async_computation.4 | async-start | bytes 8650752 | tf_op jit(solution)/shard_map/all_gather | solution.py:25
  280.6 265.7 %all-reduce.5.cloned.1.call-start = ((), (), s32[]{:S(2)}) async-start(), calls=%async_computation.5 | async-start | bytes 4194304 | tf_op jit(solution)/shard_map/psum | solution.py:40
  477.7 71.7 %copy-start.1 = (s32[32,16]{0,1:T(8,128)S(1)}, s32[32,16]{0,1:T(8,128)}, u32[]{:S(2)}) copy-start(s32[32,16]{0,1:T(8,128)} %param.10) | copy-start | bytes 6148
Sparse Core Ops, SparseCore 0:
  9.9 101.7 all-gather.2
  209.1 68.3 all-reduce.2
  280.7 99.6 all-gather.4
  477.8 68.4 all-reduce.4
where the time goes:
time: 559 us; the launch traced here: 556 us
  waiting for transfers between devices  255 us (46%)
  blocking collectives  107 us (19%)
  local copies, waits for them, and re-layouts  97.3 us (17%)
  other arithmetic  48.9 us (9%)
  matrix products  34.1 us (6%)
  between operations  13.2 us (2%)
    psum x2, waiting for transfers between devices, local(): summed = lax.psum(totals_in, 'narrow')  136 us
    all_gather x2, waiting for transfers between devices, local(): slab_rows = lax.all_gather(current, 'wide', axis=0, tiled=True)  118 us
    all_to_all x2, blocking collectives, local(): lax.all_to_all(partial_value, 'wide', split_axis=0, concat_axis=2, tiled=...  107 us
    scatter-add x1, other arithmetic, local(): tile_grid.at[tile_coords[:, 0], tile_coords[:, 1]].add(tile_values)  41.5 us
    dot_general x2, matrix products, local(): lax.dot_general(chosen, matrix, (((1,), (1,)), ((), ())), precision=lax.P...  34.1 us
    reshape x1, local copies, waits for them, and re-layouts, local(): tile_grid.transpose(0, 2, 1, 3)  18.1 us
    all_gather x2, local copies, waits for them, and re-layouts, local(): slab_rows = lax.all_gather(current, 'wide', axis=0, tiled=True)  18 us
    reshape x2, local copies, waits for them, and re-layouts, local(): slab_rows.reshape(row_count, col_blocks, tile_side)  18 us
  transfers between devices with their start and end apart: 4, of which 4 were waited for; matrix products, arithmetic and copies ran while one was open for 16% of the time, Pallas kernels for 0%

commit v1 on v0

v1 whole, which is shorter than its diff:
```python
import jax
import jax.numpy as jnp
from jax import lax
from jax.experimental import pallas as pl
from jax.experimental.pallas import tpu as pltpu
from jax.sharding import PartitionSpec as P

ITERS = 2
Z, Y, X = 8, 4, 4
NARROW = 8
SIDE = 128
ROW_BLOCKS = 16
LISTED = 16
COL_BLOCKS = 64
TILES = 192
VERTICES = 65536
EPSILON = 1e-06
MESH = pl.DeviceIdType.MESH

ORDER = (0, 2, 1, 7, 6, 4, 3, 5)
PLACE = {rel: place for place, rel in enumerate(ORDER)}
EVEN = ((0, 1), (3, 2))
ODD = ((0, 3), (1, 2))


def kernel(
    flow, tiles, where_tile, lists, masks, out,
    held, picked, chosen, left, big, small, tile_buf, partial, pair_in, pair_sum, line_in,
    reduced, own, sums, kept,
    tile_sem, z_send, z_recv, y_send, y_recv, pair_send, pair_recv, line_send, line_recv,
    own_send, own_recv, local_sem, sum_send, sum_recv,
):
    wide = lax.axis_index("wide")
    narrow = lax.axis_index("narrow")
    z, y = wide // Y, wide % Y
    x, core = narrow // 2, narrow % 2

    def device(z_at, y_at, narrow_at):
        return (((z_at + Z) % Z) * Y + (y_at + Y) % Y, narrow_at)

    is_self = (core == 0) & ((x + y) % X == 0) & (narrow == z)

    barrier = pltpu.get_barrier_semaphore()

    def greet(target):
        pl.semaphore_signal(barrier, inc=1, device_id=target, device_id_type=MESH)

    greet(device(z + 1, y, narrow))
    greet(device(z - 1, y, narrow))
    for step in range(1, Y):
        greet(device(z, y + step, narrow))
    for step in range(1, NARROW):
        greet((wide, (narrow + step) % NARROW))
    sender = (z - narrow - 2 * y + 4 * Z) % NARROW
    for y_from in range(Y):
        @pl.when(jnp.logical_not(is_self & (y == y_from)))
        def _():
            greet(device(narrow, y_from, sender))

    pieces = 4
    step_tiles = TILES // pieces
    tile_copies = [
        pltpu.make_async_copy(
            tiles.at[pl.ds(i * step_tiles, step_tiles)],
            tile_buf.at[pl.ds(i * step_tiles, step_tiles)],
            tile_sem.at[i],
        )
        for i in range(pieces)
    ]
    for copy in tile_copies:
        copy.start()
    tile_buf[TILES] = jnp.zeros((SIDE, SIDE), jnp.float32)
    for block in range(COL_BLOCKS):
        held[0][0][block] = flow[:, block * SIDE:(block + 1) * SIDE]

    @pl.when(is_self)
    def _():
        pl.semaphore_wait(barrier, 2 + 3 + 7 + 3)

    @pl.when(jnp.logical_not(is_self))
    def _():
        pl.semaphore_wait(barrier, 2 + 3 + 7 + 4)

    def expand_masks(it):
        values = masks[it].astype(jnp.float32)
        for block in range(COL_BLOCKS):
            kept[it, block] = jnp.broadcast_to(values[:, block:block + 1], (8, SIDE))

    def build(first, last):
        def one(spot, carry):
            row, slot = spot // LISTED, spot % LISTED
            tile = tile_buf[where_tile[spot]]
            high = tile.astype(jnp.bfloat16)
            low = (tile - high.astype(jnp.float32)).astype(jnp.bfloat16)
            rows = pl.ds(pl.multiple_of((row % 2) * SIDE, SIDE), SIDE)
            columns = pl.ds(pl.multiple_of(slot * SIDE, SIDE), SIDE)
            big[row // 2, rows, columns] = high
            small[row // 2, rows, columns] = low
            return carry

        lax.fori_loop(first, last, one, 0)

    for it in range(ITERS):
        y_copies = {}

        def spread(rel):
            place = PLACE[rel]
            source = held[it][rel]

            def one(slot, carry):
                for step in range(Y):
                    block = lists[z * Y + (y + step) % Y, slot]
                    if step:
                        picked[it, rel, step - 1, slot] = source[block]
                    else:
                        chosen[it, place, 0, slot] = source[block]
                return carry

            lax.fori_loop(0, LISTED, one, 0)
            for step in (1, 3, 2):
                copy = pltpu.make_async_remote_copy(
                    src_ref=picked.at[it, rel, step - 1],
                    dst_ref=chosen.at[it, place, Y - step],
                    send_sem=y_send.at[it, rel, step - 1],
                    recv_sem=y_recv.at[it, rel, step - 1],
                    device_id=device(z, y + step, narrow),
                    device_id_type=MESH,
                )
                copy.start()
                y_copies[rel, step] = copy

        z_copies = {}

        def pass_on(hop):
            for half in (0, 1):
                for way in (0, 1):
                    if hop and (hop < 4 or half == way):
                        z_copies[hop - 1, half, way].wait_recv()
                    if hop < 3 or (hop == 3 and half == way):
                        sign = -1 if way == 0 else 1
                        rows = pl.ds(half * 32, 32)
                        copy = pltpu.make_async_remote_copy(
                            src_ref=held[it][(sign * hop) % Z].at[rows],
                            dst_ref=held[it][(sign * (hop + 1)) % Z].at[rows],
                            send_sem=z_send.at[it, hop, half, way],
                            recv_sem=z_recv.at[it, hop, half, way],
                            device_id=device(z - sign, y, narrow),
                            device_id_type=MESH,
                        )
                        copy.start()
                        z_copies[hop, half, way] = copy

        def multiply(h):
            for rel in ORDER[4 * h:4 * h + 4]:
                for step in range(1, Y):
                    y_copies[rel, step].wait_recv()

            def convert(slot, carry):
                values = chosen[it, 4 * h:4 * h + 4, :, slot].reshape(SIDE, SIDE)
                high = values.astype(jnp.bfloat16)
                low = (values - high.astype(jnp.float32)).astype(jnp.bfloat16)
                columns = pl.ds(pl.multiple_of(slot * SIDE, SIDE), SIDE)
                left[0:SIDE, columns] = high
                left[SIDE:2 * SIDE, columns] = low
                return carry

            lax.fori_loop(0, LISTED, convert, 0)
            contract = (((1,), (1,)), ((), ()))

            def one(pair, carry):
                main = lax.dot_general(
                    left[...], big[pair], contract, preferred_element_type=jnp.float32
                )
                rest = lax.dot_general(
                    left[0:SIDE, :], small[pair], contract, preferred_element_type=jnp.float32
                )
                total = main[0:SIDE] + (main[SIDE:2 * SIDE] + rest)
                for side in range(2):
                    partial[it, h, :, :, 2 * pair + side] = total[
                        :, side * SIDE:(side + 1) * SIDE
                    ].reshape(4, 4, 8, SIDE)
                return carry

            lax.fori_loop(0, ROW_BLOCKS // 2, one, 0)

        def pair_copy(h):
            copy = pltpu.make_async_remote_copy(
                src_ref=partial.at[it, h, pl.ds((1 - core) * 2, 2)],
                dst_ref=pair_in.at[it, h],
                send_sem=pair_send.at[it, h],
                recv_sem=pair_recv.at[it, h],
                device_id=(wide, 2 * x + 1 - core),
                device_id_type=MESH,
            )
            copy.start()
            return copy

        def offset(h, j):
            return EVEN[h][j] + core * (ODD[h][j] - EVEN[h][j])

        def line_copies(h, paired):
            paired.wait_recv()
            copies = []
            for step in (1, 3, 2, 0):
                for j in range(2):
                    rely = (offset(h, j) - y - x - step + 4 * Y) % Y
                    pair_sum[it, h, step, j] = (
                        partial[it, h, core * 2 + j, rely] + pair_in[it, h, j, rely]
                    )
                if step:
                    copy = pltpu.make_async_remote_copy(
                        src_ref=pair_sum.at[it, h, step],
                        dst_ref=line_in.at[it, h, step - 1],
                        send_sem=line_send.at[it, h, step - 1],
                        recv_sem=line_recv.at[it, h, step - 1],
                        device_id=(wide, ((x + step) % X) * 2 + core),
                        device_id_type=MESH,
                    )
                    copy.start()
                    copies.append(copy)
            return copies

        def to_owner(h, lined):
            for copy in lined:
                copy.wait_recv()
            copies = []
            for j in range(2):
                reduced[it, h, j] = (pair_sum[it, h, 0, j] + line_in[it, h, 0, j]) + (
                    line_in[it, h, 1, j] + line_in[it, h, 2, j]
                )
                e = offset(h, j)
                rely = (e - y - x + 4 * Y) % Y
                rel = (2 * e + core) % Z
                copy = pltpu.make_async_remote_copy(
                    src_ref=reduced.at[it, h, j],
                    dst_ref=own.at[it, pl.ds(y * ROW_BLOCKS, ROW_BLOCKS)],
                    send_sem=own_send.at[it, h, j],
                    recv_sem=own_recv.at[it, y],
                    device_id=device(z + rel, y + rely, z),
                    device_id_type=MESH,
                )
                if h == 0 and j == 0:
                    @pl.when(jnp.logical_not(is_self))
                    def _():
                        copy.start()

                    @pl.when(is_self)
                    def _():
                        here = pltpu.make_async_copy(
                            reduced.at[it, h, j],
                            own.at[it, pl.ds(y * ROW_BLOCKS, ROW_BLOCKS)],
                            local_sem.at[it],
                        )
                        here.start()
                        here.wait()
                else:
                    copy.start()
                copies.append(copy)
            return copies

        pass_on(0)
        spread(0)
        if it == 0:
            for copy in tile_copies:
                copy.wait()
            build(0, 64)
        for hop in (1, 2, 3):
            pass_on(hop)
            spread(hop)
            spread(Z - hop)
            if it == 0 and hop < 3:
                build(64 + 96 * (hop - 1), 64 + 96 * hop)
        if it == 0:
            for each in range(ITERS):
                expand_masks(each)
        multiply(0)
        paired_first = pair_copy(0)
        pass_on(4)
        spread(4)
        lined_first = line_copies(0, paired_first)
        multiply(1)
        paired_second = pair_copy(1)
        sent_first = to_owner(0, lined_first)
        lined_second = line_copies(1, paired_second)
        sent_second = to_owner(1, lined_second)

        for y_from in range(Y):
            @pl.when(jnp.logical_not(is_self & (y == y_from)))
            def _():
                pltpu.make_async_remote_copy(
                    src_ref=reduced.at[it, 0, 0],
                    dst_ref=own.at[it, pl.ds(y_from * ROW_BLOCKS, ROW_BLOCKS)],
                    send_sem=own_send.at[it, 0, 0],
                    recv_sem=own_recv.at[it, y_from],
                    device_id=device(narrow, y_from, sender),
                    device_id_type=MESH,
                ).wait_recv()
        values = own[it]
        sums[it, 0] = jnp.sum(values * values, axis=0)
        sum_copies = []
        for step in range(1, NARROW):
            copy = pltpu.make_async_remote_copy(
                src_ref=sums.at[it, 0],
                dst_ref=sums.at[it, step],
                send_sem=sum_send.at[it, step - 1],
                recv_sem=sum_recv.at[it, step - 1],
                device_id=(wide, (narrow + step) % NARROW),
                device_id_type=MESH,
            )
            copy.start()
            sum_copies.append(copy)
        for copy in sum_copies:
            copy.wait_recv()
        total = jnp.sum(jnp.sum(sums[it], axis=0), axis=1, keepdims=True)
        scale = jnp.broadcast_to(total / VERTICES + EPSILON, (8, SIDE))
        for block in range(COL_BLOCKS):
            value = own[it, block]
            result = (value * value) / scale * kept[it, block]
            if it + 1 < ITERS:
                held[it + 1][0][block] = result
            else:
                out[:, block * SIDE:(block + 1) * SIDE] = result

        for copy in z_copies.values():
            copy.wait_send()
        for copy in y_copies.values():
            copy.wait_send()
        for copy in [paired_first, paired_second] + lined_first + lined_second + sum_copies:
            copy.wait_send()
        for copy in sent_first[1:] + sent_second:
            copy.wait_send()

        @pl.when(jnp.logical_not(is_self))
        def _():
            sent_first[0].wait_send()


def local(flow_panels, tile_values, tile_coords, tile_lists, keep_masks):
    spots = tile_coords[:, 0] * LISTED + tile_coords[:, 1]
    match = spots[None, :] == jnp.arange(ROW_BLOCKS * LISTED, dtype=jnp.int32)[:, None]
    index = jnp.arange(TILES, dtype=jnp.int32)[None, :]
    where_tile = jnp.min(jnp.where(match, index, TILES), axis=1)
    f32, bf16 = jnp.float32, jnp.bfloat16
    vmem = pl.BlockSpec(memory_space=pltpu.VMEM)
    smem = pl.BlockSpec(memory_space=pltpu.SMEM)
    block = (8, SIDE)
    dma = pltpu.SemaphoreType.DMA
    return pl.pallas_call(
        kernel,
        out_shape=jax.ShapeDtypeStruct(flow_panels.shape, f32),
        in_specs=[vmem, pl.BlockSpec(memory_space=pl.ANY), smem, smem, vmem],
        out_specs=vmem,
        scratch_shapes=[
            [[pltpu.VMEM((COL_BLOCKS,) + block, f32) for _ in range(Z)] for _ in range(ITERS)],
            pltpu.VMEM((ITERS, Z, Y - 1, LISTED) + block, f32),
            pltpu.VMEM((ITERS, Z, Y, LISTED) + block, f32),
            pltpu.VMEM((2 * SIDE, LISTED * SIDE), bf16),
            pltpu.VMEM((ROW_BLOCKS // 2, 2 * SIDE, LISTED * SIDE), bf16),
            pltpu.VMEM((ROW_BLOCKS // 2, 2 * SIDE, LISTED * SIDE), bf16),
            pltpu.VMEM((TILES + 1, SIDE, SIDE), f32),
            pltpu.VMEM((ITERS, 2, 4, Y, ROW_BLOCKS) + block, f32),
            pltpu.VMEM((ITERS, 2, 2, Y, ROW_BLOCKS) + block, f32),
            pltpu.VMEM((ITERS, 2, X, 2, ROW_BLOCKS) + block, f32),
            pltpu.VMEM((ITERS, 2, X - 1, 2, ROW_BLOCKS) + block, f32),
            pltpu.VMEM((ITERS, 2, 2, ROW_BLOCKS) + block, f32),
            pltpu.VMEM((ITERS, COL_BLOCKS) + block, f32),
            pltpu.VMEM((ITERS, NARROW) + block, f32),
            pltpu.VMEM((ITERS, COL_BLOCKS) + block, f32),
            dma((4,)),
            dma((ITERS, 4, 2, 2)),
            dma((ITERS, 4, 2, 2)),
            dma((ITERS, Z, Y - 1)),
            dma((ITERS, Z, Y - 1)),
            dma((ITERS, 2)),
            dma((ITERS, 2)),
            dma((ITERS, 2, X - 1)),
            dma((ITERS, 2, X - 1)),
            dma((ITERS, 2, 2)),
            dma((ITERS, Y)),
            dma((ITERS,)),
            dma((ITERS, NARROW - 1)),
            dma((ITERS, NARROW - 1)),
        ],
        compiler_params=pltpu.CompilerParams(
            collective_id=0, has_side_effects=True, vmem_limit_bytes=60 * 1024 * 1024
        ),
    )(flow_panels, tile_values, where_tile, tile_lists, keep_masks)


def solution(mesh):
    return jax.shard_map(
        local,
        mesh=mesh,
        in_specs=(
            P("wide", "narrow"),
            P(("wide", "narrow"), None, None),
            P(("wide", "narrow"), None),
            P(None, "narrow"),
            P(None, "wide", "narrow"),
        ),
        out_specs=P("wide", "narrow"),
        check_vma=False,
    )
```

time: 559 us -> 140 us (0.25)
  waiting for transfers between devices: 255 us -> 0 us
  Pallas kernels: 0 us -> 135 us
  blocking collectives: 107 us -> 0 us
  local copies, waits for them, and re-layouts: 97.3 us -> 3.05 us
  other arithmetic: 48.9 us -> 1.44 us
  matrix products: 34.1 us -> 0 us
  between operations: 13.2 us -> 0.01 us
    psum x2 -> x0, waiting for transfers between devices: 136 us -> none  [local(): summed = lax.psum(totals_in, 'narrow')]
    pallas_call x0 -> x1, Pallas kernels: none -> 135 us  [local(): pl.pallas_call(kernel, out_shape=jax.ShapeDtypeStruct(flow_panels.shape,...]
    all_gather x2 -> x0, waiting for transfers between devices: 118 us -> none  [local(): slab_rows = lax.all_gather(current, 'wide', axis=0, tiled=True)]
    all_to_all x2 -> x0, blocking collectives: 107 us -> none  [local(): lax.all_to_all(partial_value, 'wide', split_axis=0, concat_axis=2, tiled=...]
    scatter-add x1 -> x0, other arithmetic: 41.5 us -> none  [local(): tile_grid.at[tile_coords[:, 0], tile_coords[:, 1]].add(tile_values)]
    reshape x3 -> x0, local copies, waits for them, and re-layouts: 36.1 us -> none  [the longest x1 18.1 us: local(): tile_grid.transpose(0, 2, 1, 3)]
    dot_general x2 -> x0, matrix products: 34.1 us -> none  [local(): lax.dot_general(chosen, matrix, (((1,), (1,)), ((), ())), precision=lax.P...]
    all_gather x2 -> x0, local copies, waits for them, and re-layouts: 18 us -> none  [local(): slab_rows = lax.all_gather(current, 'wide', axis=0, tiled=True)]
  transfers between devices with their start and end apart: 4 -> 0, of which waited for: 4 -> 0; matrix products, arithmetic and copies ran while one was open for 16% -> 0% of each run, Pallas kernels for 0% -> 0%
where the time goes in v1:
time: 140 us
  Pallas kernels  135 us (96%)
  local copies, waits for them, and re-layouts  3.05 us (2%)
  other arithmetic  1.44 us (1%)
    pallas_call x1, Pallas kernels, local(): pl.pallas_call(kernel, out_shape=jax.ShapeDtypeStruct(flow_panels.shape,...  135 us
    unnamed x2, local copies, waits for them, and re-layouts  3.05 us

profile of v1, /device:TPU:1, one launch (start us, length us, event | category | flops | bytes accessed | tf_op | source)
XLA Modules:
  0.0 139.9 jit_solution(6601639611805027124)
XLA Ops:
  0.0 0.8 slice_add_fusion
  0.8 0.7 select_reduce_fusion.where_tile
  1.4 1.4 copy.7.lists
  2.8 135.4 %shard_map.55 = f32[8,8192]{1,0:T(8,128)} custom-call(f32[8,8192]{1,0:T(8,128)} %flow.1, f32[192,128,128]{2,1,0:T(8,128)} %tiles.1, s32[256]{0:T(256)} %select_reduce_fusion.where_tile, s32[32,16]{1,0:T(8,128)} %copy.7.lists, s32[2,8,64]{2,1,0:T(8,128)} %masks.1), custom_call_target="tpu_custom_call" | custom-call | tf_op jit(solution)/shard_map/pallas_call | solution.py:348
  138.2 1.7 %copy.9 = f32[8,8192]{1,0:T(8,128)} copy(f32[8,8192]{1,0:T(8,128)} %shard_map.55) | data formatting | bytes 524288

commit v2 on v1

v2 whole, which is shorter than its diff:
```python
import jax
import jax.numpy as jnp
from jax import lax
from jax.experimental import pallas as pl
from jax.experimental.pallas import tpu as pltpu
from jax.sharding import PartitionSpec as P

ITERS = 2
Z, Y, X = 8, 4, 4
NARROW = 8
SIDE = 128
ROW_BLOCKS = 16
LISTED = 16
COL_BLOCKS = 64
TILES = 192
VERTICES = 65536
EPSILON = 1e-06
MESH = pl.DeviceIdType.MESH

CHUNKS = ((0, 1), (2, 7), (6, 3), (4, 5))
PLACE = {rel: (c, i) for c, chunk in enumerate(CHUNKS) for i, rel in enumerate(chunk)}
ROWS = 2 * Y * 8
HALF = ROW_BLOCKS // 2


def kernel(
    flow, tiles, where_tile, lists, masks, out,
    held, picked, chosen, left, big, small, tile_buf, partial, pair_in, pair_sum, line_in,
    reduced, own, sums, kept,
    tile_sem, z_send, z_recv, y_send, y_recv, pair_send, pair_recv, line_send, line_recv,
    own_send, own_recv, local_sem, sum_send, sum_recv,
):
    wide = lax.axis_index("wide")
    narrow = lax.axis_index("narrow")
    z, y = wide // Y, wide % Y
    x, core = narrow // 2, narrow % 2

    def device(z_at, y_at, narrow_at):
        return (((z_at + Z) % Z) * Y + (y_at + Y) % Y, narrow_at)

    is_self = (core == 0) & ((x + y) % X == 0) & (narrow == z)

    barrier = pltpu.get_barrier_semaphore()

    def greet(target):
        pl.semaphore_signal(barrier, inc=1, device_id=target, device_id_type=MESH)

    greet(device(z + 1, y, narrow))
    greet(device(z - 1, y, narrow))
    for step in range(1, Y):
        greet(device(z, y + step, narrow))
    for step in range(1, NARROW):
        greet((wide, (narrow + step) % NARROW))
    sender = (z - narrow - 2 * y + 4 * Z) % NARROW
    for y_from in range(Y):
        @pl.when(jnp.logical_not(is_self & (y == y_from)))
        def _():
            greet(device(narrow, y_from, sender))

    pieces = 4
    step_tiles = TILES // pieces
    tile_copies = [
        pltpu.make_async_copy(
            tiles.at[pl.ds(i * step_tiles, step_tiles)],
            tile_buf.at[pl.ds(i * step_tiles, step_tiles)],
            tile_sem.at[i],
        )
        for i in range(pieces)
    ]
    for copy in tile_copies:
        copy.start()
    tile_buf[TILES] = jnp.zeros((SIDE, SIDE), jnp.float32)
    for block in range(COL_BLOCKS):
        held[0][0][block] = flow[:, block * SIDE:(block + 1) * SIDE]

    @pl.when(is_self)
    def _():
        pl.semaphore_wait(barrier, 2 + 3 + 7 + 3)

    @pl.when(jnp.logical_not(is_self))
    def _():
        pl.semaphore_wait(barrier, 2 + 3 + 7 + 4)

    def expand_masks(it):
        values = masks[it].astype(jnp.float32)
        for block in range(COL_BLOCKS):
            kept[it, block] = jnp.broadcast_to(values[:, block:block + 1], (8, SIDE))

    def build(first, last):
        def one(spot, carry):
            row, slot = spot // LISTED, spot % LISTED
            tile = tile_buf[where_tile[spot]].T
            high = tile.astype(jnp.bfloat16)
            low = (tile - high.astype(jnp.float32)).astype(jnp.bfloat16)
            rows = pl.ds(pl.multiple_of(slot * SIDE, SIDE), SIDE)
            columns = pl.ds(pl.multiple_of((row % 2) * SIDE, SIDE), SIDE)
            big[row // 2, rows, columns] = high
            small[row // 2, rows, columns] = low
            return carry

        lax.fori_loop(first, last, one, 0, unroll=4)

    leaving, leaving_apart = [], []
    for it in range(ITERS):
        y_copies = {}
        extra = min(it, 1)

        def spread(rel):
            c, place = PLACE[rel]
            source = held[it][rel]

            def one(slot, carry):
                for step in range(Y):
                    block = lists[z * Y + (y + step) % Y, slot]
                    if step:
                        picked[it, rel, step - 1, slot] = source[block]
                    else:
                        chosen[it, c, place, 0, slot] = source[block]
                return carry

            lax.fori_loop(0, LISTED, one, 0)
            sent_blocks = pl.ds(0, LISTED + extra)
            if extra:
                chosen[it, c, place, 0, LISTED] = source[COL_BLOCKS]
            for step in (2, 1, 3):
                if extra:
                    picked[it, rel, step - 1, LISTED] = source[COL_BLOCKS]
                copy = pltpu.make_async_remote_copy(
                    src_ref=picked.at[it, rel, step - 1, sent_blocks],
                    dst_ref=chosen.at[it, c, place, Y - step, sent_blocks],
                    send_sem=y_send.at[it, rel, step - 1],
                    recv_sem=y_recv.at[it, rel, step - 1],
                    device_id=device(z, y + step, narrow),
                    device_id_type=MESH,
                )
                copy.start()
                y_copies[rel, step] = copy

        z_copies = {}

        def pass_on(hop, halves=(0, 1)):
            for half in halves:
                for way in (0, 1):
                    if hop and (hop < 4 or half == way):
                        z_copies[hop - 1, half, way].wait_recv()
                    if hop < 3 or (hop == 3 and half == way):
                        sign = -1 if way == 0 else 1
                        rows = pl.ds(half * 32, 32 + half * extra)
                        copy = pltpu.make_async_remote_copy(
                            src_ref=held[it][(sign * hop) % Z].at[rows],
                            dst_ref=held[it][(sign * (hop + 1)) % Z].at[rows],
                            send_sem=z_send.at[it, hop, half, way],
                            recv_sem=z_recv.at[it, hop, half, way],
                            device_id=device(z - sign, y, narrow),
                            device_id_type=MESH,
                        )
                        copy.start()
                        z_copies[hop, half, way] = copy

        def arrive(c):
            for rel in CHUNKS[c]:
                for step in range(1, Y):
                    y_copies[rel, step].wait_recv()

            if extra:
                scales = chosen[it, c, :, :, LISTED].reshape(ROWS, SIDE)

            def convert(slot, carry):
                values = chosen[it, c, :, :, slot].reshape(ROWS, SIDE)
                if extra:
                    values = values / scales
                high = values.astype(jnp.bfloat16)
                low = (values - high.astype(jnp.float32)).astype(jnp.bfloat16)
                columns = pl.ds(pl.multiple_of(slot * SIDE, SIDE), SIDE)
                left[0:ROWS, columns] = high
                left[ROWS:2 * ROWS, columns] = low
                return carry

            lax.fori_loop(0, LISTED, convert, 0)

        def multiply(c, first=0, last=ROW_BLOCKS // 2):
            def one(pair, carry):
                main = jnp.dot(left[...], big[pair], preferred_element_type=jnp.float32)
                rest = jnp.dot(left[0:ROWS, :], small[pair], preferred_element_type=jnp.float32)
                total = main[0:ROWS] + (main[ROWS:2 * ROWS] + rest)
                for side in range(2):
                    partial[it, c, :, :, 2 * pair + side] = total[
                        :, side * SIDE:(side + 1) * SIDE
                    ].reshape(2, Y, 8, SIDE)
                return carry

            lax.fori_loop(first, last, one, 0)

        def pair_copy(c, part):
            rows = pl.ds(part * HALF, HALF)
            copy = pltpu.make_async_remote_copy(
                src_ref=partial.at[it, c, 1 - core, :, rows],
                dst_ref=pair_in.at[it, c, :, rows],
                send_sem=pair_send.at[it, c, part],
                recv_sem=pair_recv.at[it, c, part],
                device_id=(wide, 2 * x + 1 - core),
                device_id_type=MESH,
            )
            copy.start()
            paired[c, part] = copy

        def offset(c):
            even, odd = CHUNKS[c][0] // 2, CHUNKS[c][1] // 2
            return even + core * (odd - even)

        def line_copies(c, part):
            paired[c, part].wait_recv()
            lined[c, part] = []
            rows = pl.ds(part * HALF, HALF)
            for step in (2, 1, 3, 0):
                rely = (offset(c) - y - x - step + 4 * Y) % Y
                pair_sum[it, c, step, rows] = (
                    partial[it, c, core, rely, rows] + pair_in[it, c, rely, rows]
                )
                if step:
                    copy = pltpu.make_async_remote_copy(
                        src_ref=pair_sum.at[it, c, step, rows],
                        dst_ref=line_in.at[it, c, step - 1, rows],
                        send_sem=line_send.at[it, c, step - 1, part],
                        recv_sem=line_recv.at[it, c, step - 1, part],
                        device_id=(wide, ((x + step) % X) * 2 + core),
                        device_id_type=MESH,
                    )
                    copy.start()
                    lined[c, part].append(copy)

        def to_owner(c, part):
            for copy in lined[c, part]:
                copy.wait_recv()
            rows = pl.ds(part * HALF, HALF)
            reduced[it, c, rows] = (pair_sum[it, c, 0, rows] + line_in[it, c, 0, rows]) + (
                line_in[it, c, 1, rows] + line_in[it, c, 2, rows]
            )
            rely = (offset(c) - y - x + 4 * Y) % Y
            rel = (2 * offset(c) + core) % Z
            place = own.at[it, pl.ds(y * ROW_BLOCKS + part * HALF, HALF)]
            copy = pltpu.make_async_remote_copy(
                src_ref=reduced.at[it, c, rows],
                dst_ref=place,
                send_sem=own_send.at[it, c, part],
                recv_sem=own_recv.at[it, y, part],
                device_id=device(z + rel, y + rely, z),
                device_id_type=MESH,
            )
            if c == 0:
                @pl.when(jnp.logical_not(is_self))
                def _():
                    copy.start()

                @pl.when(is_self)
                def _():
                    here = pltpu.make_async_copy(
                        reduced.at[it, c, rows], place, local_sem.at[it, part]
                    )
                    here.start()
                    here.wait()
            else:
                copy.start()
            sent[c, part] = copy

        paired, lined, sent = {}, {}, {}
        if it == 0:
            pass_on(0)
        else:
            pass_on(0, (0,))
            held[it][0][COL_BLOCKS] = scale_of(it - 1)
            pass_on(0, (1,))
        spread(0)
        if it == 0:
            for copy in tile_copies:
                copy.wait()
            build(0, 80)
        pass_on(1)
        spread(1)
        spread(7)
        if it == 0:
            build(80, 176)
        pass_on(2)
        spread(2)
        spread(6)
        if it == 0:
            build(176, 256)
        arrive(0)
        multiply(0, 0, 4)
        pass_on(3, (0,))
        multiply(0, 4, 8)
        pair_copy(0, 0)
        pair_copy(0, 1)
        pass_on(3, (1,))
        spread(3)
        spread(5)
        arrive(1)
        multiply(1)
        pair_copy(1, 0)
        pair_copy(1, 1)
        pass_on(4)
        spread(4)
        line_copies(0, 0)
        line_copies(0, 1)
        arrive(2)
        multiply(2)
        pair_copy(2, 0)
        pair_copy(2, 1)
        line_copies(1, 0)
        line_copies(1, 1)
        to_owner(0, 0)
        to_owner(0, 1)
        arrive(3)
        line_copies(2, 0)
        line_copies(2, 1)
        multiply(3, 0, 4)
        pair_copy(3, 0)
        to_owner(1, 0)
        to_owner(1, 1)
        multiply(3, 4, 6)
        line_copies(3, 0)
        multiply(3, 6, 8)
        pair_copy(3, 1)
        to_owner(2, 0)
        to_owner(2, 1)
        line_copies(3, 1)
        to_owner(3, 0)
        expand_masks(it)
        to_owner(3, 1)

        for y_from in range(Y):
            @pl.when(jnp.logical_not(is_self & (y == y_from)))
            def _():
                for part in range(2):
                    pltpu.make_async_remote_copy(
                        src_ref=reduced.at[it, 0, pl.ds(part * HALF, HALF)],
                        dst_ref=own.at[it, pl.ds(y_from * ROW_BLOCKS + part * HALF, HALF)],
                        send_sem=own_send.at[it, 0, part],
                        recv_sem=own_recv.at[it, y_from, part],
                        device_id=device(narrow, y_from, sender),
                        device_id_type=MESH,
                    ).wait_recv()
        values = own[it]
        sums[it, 0] = jnp.sum(values * values, axis=0)
        sum_copies = []
        for step in range(1, NARROW):
            copy = pltpu.make_async_remote_copy(
                src_ref=sums.at[it, 0],
                dst_ref=sums.at[it, step],
                send_sem=sum_send.at[it, step - 1],
                recv_sem=sum_recv.at[it, step - 1],
                device_id=(wide, (narrow + step) % NARROW),
                device_id_type=MESH,
            )
            copy.start()
            sum_copies.append(copy)

        def scale_of(at, copies=sum_copies):
            for copy in copies:
                copy.wait_recv()
            total = jnp.sum(jnp.sum(sums[at], axis=0), axis=1, keepdims=True)
            return jnp.broadcast_to(total / VERTICES + EPSILON, (8, SIDE))

        if it + 1 < ITERS:
            for block in range(COL_BLOCKS):
                value = own[it, block]
                held[it + 1][0][block] = (value * value) * kept[it, block]
        else:
            scale = scale_of(it)
            for block in range(COL_BLOCKS):
                value = own[it, block]
                out[:, block * SIDE:(block + 1) * SIDE] = (value * value) / scale * kept[it, block]

        leaving.extend(z_copies.values())
        leaving.extend(y_copies.values())
        leaving.extend(paired.values())
        leaving.extend(sum(lined.values(), []))
        leaving.extend(sum_copies)
        for (c, part), copy in sent.items():
            (leaving if c else leaving_apart).append(copy)

    for copy in leaving:
        copy.wait_send()

    @pl.when(jnp.logical_not(is_self))
    def _():
        for copy in leaving_apart:
            copy.wait_send()


def local(flow_panels, tile_values, tile_coords, tile_lists, keep_masks):
    spots = tile_coords[:, 0] * LISTED + tile_coords[:, 1]
    match = spots[None, :] == jnp.arange(ROW_BLOCKS * LISTED, dtype=jnp.int32)[:, None]
    index = jnp.arange(TILES, dtype=jnp.int32)[None, :]
    where_tile = jnp.min(jnp.where(match, index, TILES), axis=1)
    f32, bf16 = jnp.float32, jnp.bfloat16
    vmem = pl.BlockSpec(memory_space=pltpu.VMEM)
    smem = pl.BlockSpec(memory_space=pltpu.SMEM)
    block = (8, SIDE)
    dma = pltpu.SemaphoreType.DMA
    return pl.pallas_call(
        kernel,
        out_shape=jax.ShapeDtypeStruct(flow_panels.shape, f32),
        in_specs=[vmem, pl.BlockSpec(memory_space=pl.ANY), smem, smem, vmem],
        out_specs=vmem,
        scratch_shapes=[
            [
                [pltpu.VMEM((COL_BLOCKS + min(it, 1),) + block, f32) for _ in range(Z)]
                for it in range(ITERS)
            ],
            pltpu.VMEM((ITERS, Z, Y - 1, LISTED + 1) + block, f32),
            pltpu.VMEM((ITERS, 4, 2, Y, LISTED + 1) + block, f32),
            pltpu.VMEM((2 * ROWS, LISTED * SIDE), bf16),
            pltpu.VMEM((ROW_BLOCKS // 2, LISTED * SIDE, 2 * SIDE), bf16),
            pltpu.VMEM((ROW_BLOCKS // 2, LISTED * SIDE, 2 * SIDE), bf16),
            pltpu.VMEM((TILES + 1, SIDE, SIDE), f32),
            pltpu.VMEM((ITERS, 4, 2, Y, ROW_BLOCKS) + block, f32),
            pltpu.VMEM((ITERS, 4, Y, ROW_BLOCKS) + block, f32),
            pltpu.VMEM((ITERS, 4, X, ROW_BLOCKS) + block, f32),
            pltpu.VMEM((ITERS, 4, X - 1, ROW_BLOCKS) + block, f32),
            pltpu.VMEM((ITERS, 4, ROW_BLOCKS) + block, f32),
            pltpu.VMEM((ITERS, COL_BLOCKS) + block, f32),
            pltpu.VMEM((ITERS, NARROW) + block, f32),
            pltpu.VMEM((ITERS, COL_BLOCKS) + block, f32),
            dma((4,)),
            dma((ITERS, 4, 2, 2)),
            dma((ITERS, 4, 2, 2)),
            dma((ITERS, Z, Y - 1)),
            dma((ITERS, Z, Y - 1)),
            dma((ITERS, 4, 2)),
            dma((ITERS, 4, 2)),
            dma((ITERS, 4, X - 1, 2)),
            dma((ITERS, 4, X - 1, 2)),
            dma((ITERS, 4, 2)),
            dma((ITERS, Y, 2)),
            dma((ITERS, 2)),
            dma((ITERS, NARROW - 1)),
            dma((ITERS, NARROW - 1)),
        ],
        compiler_params=pltpu.CompilerParams(
            collective_id=0, has_side_effects=True, vmem_limit_bytes=60 * 1024 * 1024
        ),
    )(flow_panels, tile_values, where_tile, tile_lists, keep_masks)


def solution(mesh):
    return jax.shard_map(
        local,
        mesh=mesh,
        in_specs=(
            P("wide", "narrow"),
            P(("wide", "narrow"), None, None),
            P(("wide", "narrow"), None),
            P(None, "narrow"),
            P(None, "wide", "narrow"),
        ),
        out_specs=P("wide", "narrow"),
        check_vma=False,
    )
```

time: 140 us -> 128 us (0.914)
  Pallas kernels: 135 us -> 123 us
    pallas_call x1, Pallas kernels: 135 us -> 123 us  [local(): pl.pallas_call(kernel, out_shape=jax.ShapeDtypeStruct(flow_panels.shape,...]
where the time goes in v2:
time: 128 us; the launch traced here: 127 us
  Pallas kernels  123 us (96%)
  local copies, waits for them, and re-layouts  3.05 us (2%)
  other arithmetic  1.44 us (1%)
    pallas_call x1, Pallas kernels, local(): pl.pallas_call(kernel, out_shape=jax.ShapeDtypeStruct(flow_panels.shape,...  123 us
    unnamed x2, local copies, waits for them, and re-layouts  3.05 us

profile of v2, /device:TPU:1, one launch (start us, length us, event | category | flops | bytes accessed | tf_op | source)
XLA Modules:
  0.0 127.3 jit_solution(16550898223900748211)
XLA Ops:
  0.0 0.8 slice_add_fusion
  0.8 0.7 select_reduce_fusion.where_tile
  1.4 1.4 %copy.7.lists = s32[32,16]{1,0:T(8,128)} copy(s32[32,16]{0,1:T(8,128)} %param.8) | data formatting | bytes 4096 | tf_op args[3]
  2.8 122.8 %shard_map.55 = f32[8,8192]{1,0:T(8,128)} custom-call(f32[8,8192]{1,0:T(8,128)} %flow.1, f32[192,128,128]{2,1,0:T(8,128)} %tiles.1, s32[256]{0:T(256)} %select_reduce_fusion.where_tile, s32[32,16]{1,0:T(8,128)} %copy.7.lists, s32[2,8,64]{2,1,0:T(8,128)} %masks.1), custom_call_target="tpu_custom_call" | custom-call | tf_op jit(solution)/shard_map/pallas_call | solution.py:401
  125.6 1.7 %copy.9 = f32[8,8192]{1,0:T(8,128)} copy(f32[8,8192]{1,0:T(8,128)} %shard_map.55) | data formatting | bytes 524288

commit v3 on v2

--- a/solution.py
+++ b/solution.py
@@ -24,10 +24,10 @@
 
 
 def kernel(
-    flow, tiles, where_tile, lists, masks, out,
+    flow, tiles, coords, lists, masks, out, where_tile, where_rows,
     held, picked, chosen, left, big, small, tile_buf, partial, pair_in, pair_sum, line_in,
     reduced, own, sums, kept,
-    tile_sem, z_send, z_recv, y_send, y_recv, pair_send, pair_recv, line_send, line_recv,
+    where_sem, tile_sem, z_send, z_recv, y_send, y_recv, pair_send, pair_recv, line_send, line_recv,
     own_send, own_recv, local_sem, sum_send, sum_recv,
 ):
     wide = lax.axis_index("wide")
@@ -52,10 +52,6 @@
     for step in range(1, NARROW):
         greet((wide, (narrow + step) % NARROW))
     sender = (z - narrow - 2 * y + 4 * Z) % NARROW
-    for y_from in range(Y):
-        @pl.when(jnp.logical_not(is_self & (y == y_from)))
-        def _():
-            greet(device(narrow, y_from, sender))
 
     pieces = 4
     step_tiles = TILES // pieces
@@ -69,17 +65,19 @@
     ]
     for copy in tile_copies:
         copy.start()
+    spots = coords[0:1, :] * LISTED + coords[1:2, :]
+    grid = (ROW_BLOCKS * LISTED, TILES)
+    match = lax.broadcasted_iota(jnp.int32, grid, 0) == spots
+    index = jnp.where(match, lax.broadcasted_iota(jnp.int32, grid, 1), TILES)
+    where_rows[...] = jnp.broadcast_to(
+        jnp.min(index, axis=1, keepdims=True), (ROW_BLOCKS * LISTED, SIDE)
+    )
+    where_copy = pltpu.make_async_copy(where_rows, where_tile, where_sem)
+    where_copy.start()
     tile_buf[TILES] = jnp.zeros((SIDE, SIDE), jnp.float32)
     for block in range(COL_BLOCKS):
         held[0][0][block] = flow[:, block * SIDE:(block + 1) * SIDE]
-
-    @pl.when(is_self)
-    def _():
-        pl.semaphore_wait(barrier, 2 + 3 + 7 + 3)
-
-    @pl.when(jnp.logical_not(is_self))
-    def _():
-        pl.semaphore_wait(barrier, 2 + 3 + 7 + 4)
+    pl.semaphore_wait(barrier, 2 + (Y - 1) + (NARROW - 1))
 
     def expand_masks(it):
         values = masks[it].astype(jnp.float32)
@@ -89,7 +87,7 @@
     def build(first, last):
         def one(spot, carry):
             row, slot = spot // LISTED, spot % LISTED
-            tile = tile_buf[where_tile[spot]].T
+            tile = tile_buf[where_tile[spot, 0]].T
             high = tile.astype(jnp.bfloat16)
             low = (tile - high.astype(jnp.float32)).astype(jnp.bfloat16)
             rows = pl.ds(pl.multiple_of(slot * SIDE, SIDE), SIDE)
@@ -111,7 +109,7 @@
 
             def one(slot, carry):
                 for step in range(Y):
-                    block = lists[z * Y + (y + step) % Y, slot]
+                    block = lists[slot, z * Y + (y + step) % Y]
                     if step:
                         picked[it, rel, step - 1, slot] = source[block]
                     else:
@@ -272,51 +270,70 @@
             pass_on(0, (1,))
         spread(0)
         if it == 0:
+            where_copy.wait()
             for copy in tile_copies:
                 copy.wait()
-            build(0, 80)
-        pass_on(1)
+            build(0, 32)
+        pass_on(1, (0,))
+        if it == 0:
+            build(32, 64)
+        pass_on(1, (1,))
         spread(1)
         spread(7)
         if it == 0:
-            build(80, 176)
-        pass_on(2)
+            build(64, 108)
+        pass_on(2, (0,))
+        if it == 0:
+            build(108, 152)
+        pass_on(2, (1,))
         spread(2)
         spread(6)
         if it == 0:
-            build(176, 256)
-        arrive(0)
-        multiply(0, 0, 4)
-        pass_on(3, (0,))
-        multiply(0, 4, 8)
-        pair_copy(0, 0)
-        pair_copy(0, 1)
-        pass_on(3, (1,))
+            build(152, 204)
+            pass_on(3, (0,))
+            build(204, 256)
+            pass_on(3, (1,))
+        else:
+            arrive(0)
+            multiply(0, 0, 4)
+            pass_on(3, (0,))
+            multiply(0, 4, 8)
+            pair_copy(0, 0)
+            pair_copy(0, 1)
+            pass_on(3, (1,))
         spread(3)
         spread(5)
+        if it == 0:
+            arrive(0)
+            multiply(0)
+            pair_copy(0, 0)
+            pair_copy(0, 1)
+            pass_on(4)
+            spread(4)
+        line_copies(0, 0)
+        line_copies(0, 1)
         arrive(1)
         multiply(1)
         pair_copy(1, 0)
         pair_copy(1, 1)
-        pass_on(4)
-        spread(4)
-        line_copies(0, 0)
-        line_copies(0, 1)
+        if it:
+            pass_on(4)
+            spread(4)
+        line_copies(1, 0)
+        line_copies(1, 1)
+        to_owner(0, 0)
+        to_owner(0, 1)
         arrive(2)
         multiply(2)
         pair_copy(2, 0)
         pair_copy(2, 1)
-        line_copies(1, 0)
-        line_copies(1, 1)
-        to_owner(0, 0)
-        to_owner(0, 1)
-        arrive(3)
+        to_owner(1, 0)
+        to_owner(1, 1)
         line_copies(2, 0)
         line_copies(2, 1)
+        arrive(3)
         multiply(3, 0, 4)
         pair_copy(3, 0)
-        to_owner(1, 0)
-        to_owner(1, 1)
         multiply(3, 4, 6)
         line_copies(3, 0)
         multiply(3, 6, 8)
@@ -325,7 +342,8 @@
         to_owner(2, 1)
         line_copies(3, 1)
         to_owner(3, 0)
-        expand_masks(it)
+        if it + 1 < ITERS:
+            expand_masks(it)
         to_owner(3, 1)
 
         for y_from in range(Y):
@@ -369,7 +387,7 @@
             scale = scale_of(it)
             for block in range(COL_BLOCKS):
                 value = own[it, block]
-                out[:, block * SIDE:(block + 1) * SIDE] = (value * value) / scale * kept[it, block]
+                out[:, block * SIDE:(block + 1) * SIDE] = (value * value) / scale
 
         leaving.extend(z_copies.values())
         leaving.extend(y_copies.values())
@@ -389,21 +407,19 @@
 
 
 def local(flow_panels, tile_values, tile_coords, tile_lists, keep_masks):
-    spots = tile_coords[:, 0] * LISTED + tile_coords[:, 1]
-    match = spots[None, :] == jnp.arange(ROW_BLOCKS * LISTED, dtype=jnp.int32)[:, None]
-    index = jnp.arange(TILES, dtype=jnp.int32)[None, :]
-    where_tile = jnp.min(jnp.where(match, index, TILES), axis=1)
     f32, bf16 = jnp.float32, jnp.bfloat16
     vmem = pl.BlockSpec(memory_space=pltpu.VMEM)
     smem = pl.BlockSpec(memory_space=pltpu.SMEM)
     block = (8, SIDE)
     dma = pltpu.SemaphoreType.DMA
-    return pl.pallas_call(
+    scaled = pl.pallas_call(
         kernel,
         out_shape=jax.ShapeDtypeStruct(flow_panels.shape, f32),
-        in_specs=[vmem, pl.BlockSpec(memory_space=pl.ANY), smem, smem, vmem],
+        in_specs=[vmem, pl.BlockSpec(memory_space=pl.ANY), vmem, smem, vmem],
         out_specs=vmem,
         scratch_shapes=[
+            pltpu.SMEM((ROW_BLOCKS * LISTED, SIDE), jnp.int32),
+            pltpu.VMEM((ROW_BLOCKS * LISTED, SIDE), jnp.int32),
             [
                 [pltpu.VMEM((COL_BLOCKS + min(it, 1),) + block, f32) for _ in range(Z)]
                 for it in range(ITERS)
@@ -422,6 +438,7 @@
             pltpu.VMEM((ITERS, COL_BLOCKS) + block, f32),
             pltpu.VMEM((ITERS, NARROW) + block, f32),
             pltpu.VMEM((ITERS, COL_BLOCKS) + block, f32),
+            dma,
             dma((4,)),
             dma((ITERS, 4, 2, 2)),
             dma((ITERS, 4, 2, 2)),
@@ -440,7 +457,11 @@
         compiler_params=pltpu.CompilerParams(
             collective_id=0, has_side_effects=True, vmem_limit_bytes=60 * 1024 * 1024
         ),
-    )(flow_panels, tile_values, where_tile, tile_lists, keep_masks)
+    )(flow_panels, tile_values, tile_coords.T, tile_lists.T, keep_masks)
+    rows, width = scaled.shape
+    last = keep_masks[ITERS - 1].astype(f32)
+    blocks = scaled.reshape(rows, width // SIDE, SIDE) * last[:, :, None]
+    return blocks.reshape(rows, width)
 
 
 def solution(mesh):

time: 128 us -> 123 us (0.961)
  Pallas kernels: 123 us -> 120 us
  local copies, waits for them, and re-layouts: 3.05 us -> 0.09 us
    unnamed x2 -> x0, local copies, waits for them, and re-layouts: 3.05 us -> none
    pallas_call x1, Pallas kernels: 123 us -> 120 us  [local(): pl.pallas_call(kernel, out_shape=jax.ShapeDtypeStruct(flow_panels.shape,...]
    mul x0 -> x1, other arithmetic: none -> 1.79 us  [local(): blocks = scaled.reshape(rows, width // SIDE, SIDE) * last[:, :, None]]
where the time goes in v3:
time: 123 us
  Pallas kernels  120 us (98%)
  other arithmetic  2.48 us (2%)
    pallas_call x1, Pallas kernels, local(): pl.pallas_call(kernel, out_shape=jax.ShapeDtypeStruct(flow_panels.shape,...  120 us

profile of v3, /device:TPU:1, one launch (start us, length us, event | category | flops | bytes accessed | tf_op | source)
XLA Modules:
  0.0 122.8 jit_solution(16665179178292385754)
XLA Ops:
  0.0 0.7 convert_bitcast_fusion
  0.7 0.1 copy.6
  0.8 120.2 %shard_map.55 = f32[8,8192]{1,0:T(8,128)} custom-call(f32[8,8192]{1,0:T(8,128)} %flow.1, f32[192,128,128]{2,1,0:T(8,128)} %tiles.1, s32[2,192]{1,0:T(2,128)} %bitcast.7, s32[16,32]{1,0:T(8,128)} %bitcast.6, s32[2,8,64]{2,1,0:T(8,128)} %masks.1), custom_call_target="tpu_custom_call" | custom-call | tf_op jit(solution)/shard_map/pallas_call | solution.py:415
  121.0 1.8 %bitcast_multiply_fusion = f32[8,8192]{1,0:T(8,128)} fusion(f32[8,8192]{1,0:T(8,128)} %shard_map.55, f32[8,64]{0,1:T(8,128)S(1)} %copy.6), kind=kLoop, calls=%fused_computation | loop fusion | flops 65536 | bytes 526336 | tf_op jit(solution)/shard_map/mul | solution.py:463

commit v4 on v3

--- a/solution.py
+++ b/solution.py
@@ -116,7 +116,7 @@
                         chosen[it, c, place, 0, slot] = source[block]
                 return carry
 
-            lax.fori_loop(0, LISTED, one, 0)
+            lax.fori_loop(0, LISTED, one, 0, unroll=4)
             sent_blocks = pl.ds(0, LISTED + extra)
             if extra:
                 chosen[it, c, place, 0, LISTED] = source[COL_BLOCKS]
@@ -136,14 +136,17 @@
 
         z_copies = {}
 
-        def pass_on(hop, halves=(0, 1)):
-            for half in halves:
+        def pass_on(hop, pieces=(0, 1, 2)):
+            for half in pieces[:len(pieces) if extra else 2]:
+                if half == 2 and not extra:
+                    continue
                 for way in (0, 1):
-                    if hop and (hop < 4 or half == way):
+                    last = way == half % 2
+                    if hop and (hop < 4 or last):
                         z_copies[hop - 1, half, way].wait_recv()
-                    if hop < 3 or (hop == 3 and half == way):
+                    if hop < 3 or (hop == 3 and last):
                         sign = -1 if way == 0 else 1
-                        rows = pl.ds(half * 32, 32 + half * extra)
+                        rows = pl.ds(half * 32, 1 if half == 2 else 32)
                         copy = pltpu.make_async_remote_copy(
                             src_ref=held[it][(sign * hop) % Z].at[rows],
                             dst_ref=held[it][(sign * (hop + 1)) % Z].at[rows],
@@ -174,7 +177,7 @@
                 left[ROWS:2 * ROWS, columns] = low
                 return carry
 
-            lax.fori_loop(0, LISTED, convert, 0)
+            lax.fori_loop(0, LISTED, convert, 0, unroll=4)
 
         def multiply(c, first=0, last=ROW_BLOCKS // 2):
             def one(pair, carry):
@@ -187,7 +190,7 @@
                     ].reshape(2, Y, 8, SIDE)
                 return carry
 
-            lax.fori_loop(first, last, one, 0)
+            lax.fori_loop(first, last, one, 0, unroll=2)
 
         def pair_copy(c, part):
             rows = pl.ds(part * HALF, HALF)
@@ -265,9 +268,9 @@
         if it == 0:
             pass_on(0)
         else:
-            pass_on(0, (0,))
+            pass_on(0, (0, 1))
             held[it][0][COL_BLOCKS] = scale_of(it - 1)
-            pass_on(0, (1,))
+            pass_on(0, (2,))
         spread(0)
         if it == 0:
             where_copy.wait()
@@ -277,7 +280,7 @@
         pass_on(1, (0,))
         if it == 0:
             build(32, 64)
-        pass_on(1, (1,))
+        pass_on(1, (1, 2))
         spread(1)
         spread(7)
         if it == 0:
@@ -285,14 +288,14 @@
         pass_on(2, (0,))
         if it == 0:
             build(108, 152)
-        pass_on(2, (1,))
+        pass_on(2, (1, 2))
         spread(2)
         spread(6)
         if it == 0:
             build(152, 204)
             pass_on(3, (0,))
             build(204, 256)
-            pass_on(3, (1,))
+            pass_on(3, (1, 2))
         else:
             arrive(0)
             multiply(0, 0, 4)
@@ -300,7 +303,7 @@
             multiply(0, 4, 8)
             pair_copy(0, 0)
             pair_copy(0, 1)
-            pass_on(3, (1,))
+            pass_on(3, (1, 2))
         spread(3)
         spread(5)
         if it == 0:
@@ -342,8 +345,7 @@
         to_owner(2, 1)
         line_copies(3, 1)
         to_owner(3, 0)
-        if it + 1 < ITERS:
-            expand_masks(it)
+        expand_masks(it)
         to_owner(3, 1)
 
         for y_from in range(Y):
@@ -387,7 +389,7 @@
             scale = scale_of(it)
             for block in range(COL_BLOCKS):
                 value = own[it, block]
-                out[:, block * SIDE:(block + 1) * SIDE] = (value * value) / scale
+                out[:, block * SIDE:(block + 1) * SIDE] = (value * value) / scale * kept[it, block]
 
         leaving.extend(z_copies.values())
         leaving.extend(y_copies.values())
@@ -412,7 +414,7 @@
     smem = pl.BlockSpec(memory_space=pltpu.SMEM)
     block = (8, SIDE)
     dma = pltpu.SemaphoreType.DMA
-    scaled = pl.pallas_call(
+    return pl.pallas_call(
         kernel,
         out_shape=jax.ShapeDtypeStruct(flow_panels.shape, f32),
         in_specs=[vmem, pl.BlockSpec(memory_space=pl.ANY), vmem, smem, vmem],
@@ -440,8 +442,8 @@
             pltpu.VMEM((ITERS, COL_BLOCKS) + block, f32),
             dma,
             dma((4,)),
-            dma((ITERS, 4, 2, 2)),
-            dma((ITERS, 4, 2, 2)),
+            dma((ITERS, 4, 3, 2)),
+            dma((ITERS, 4, 3, 2)),
             dma((ITERS, Z, Y - 1)),
             dma((ITERS, Z, Y - 1)),
             dma((ITERS, 4, 2)),
@@ -458,10 +460,6 @@
             collective_id=0, has_side_effects=True, vmem_limit_bytes=60 * 1024 * 1024
         ),
     )(flow_panels, tile_values, tile_coords.T, tile_lists.T, keep_masks)
-    rows, width = scaled.shape
-    last = keep_masks[ITERS - 1].astype(f32)
-    blocks = scaled.reshape(rows, width // SIDE, SIDE) * last[:, :, None]
-    return blocks.reshape(rows, width)
 
 
 def solution(mesh):

time: 123 us -> 120 us (0.976)
  Pallas kernels: 120 us -> 117 us
  other arithmetic: 2.48 us -> 0 us
  local copies, waits for them, and re-layouts: 0.09 us -> 1.67 us
    pallas_call x1, Pallas kernels: 120 us -> 117 us  [local(): pl.pallas_call(kernel, out_shape=jax.ShapeDtypeStruct(flow_panels.shape,...]
    mul x1 -> x0, other arithmetic: 1.79 us -> none  [local(): blocks = scaled.reshape(rows, width // SIDE, SIDE) * last[:, :, None]]
    unnamed x0 -> x1, local copies, waits for them, and re-layouts: none -> 1.67 us
where the time goes in v4:
time: 120 us; the launch traced here: 119 us
  Pallas kernels  117 us (98%)
  local copies, waits for them, and re-layouts  1.67 us (1%)
    pallas_call x1, Pallas kernels, local(): pl.pallas_call(kernel, out_shape=jax.ShapeDtypeStruct(flow_panels.shape,...  117 us

profile of v4, /device:TPU:1, one launch (start us, length us, event | category | flops | bytes accessed | tf_op | source)
XLA Modules:
  0.0 118.8 jit_solution(8561070859356668231)
XLA Ops:
  0.0 117.1 %shard_map.55 = f32[8,8192]{1,0:T(8,128)} custom-call(f32[8,8192]{1,0:T(8,128)} %flow.1, f32[192,128,128]{2,1,0:T(8,128)} %tiles.1, s32[2,192]{1,0:T(2,128)} %bitcast.3, s32[16,32]{1,0:T(8,128)} %bitcast.2, s32[2,8,64]{2,1,0:T(8,128)} %masks.1), custom_call_target="tpu_custom_call" | custom-call | tf_op jit(solution)/shard_map/pallas_call | solution.py:417
  117.2 1.7 %copy.7 = f32[8,8192]{1,0:T(8,128)} copy(f32[8,8192]{1,0:T(8,128)} %shard_map.55) | data formatting | bytes 524288

commit v5 on v4

--- a/solution.py
+++ b/solution.py
@@ -116,7 +116,7 @@
                         chosen[it, c, place, 0, slot] = source[block]
                 return carry
 
-            lax.fori_loop(0, LISTED, one, 0, unroll=4)
+            lax.fori_loop(0, LISTED, one, 0, unroll=8)
             sent_blocks = pl.ds(0, LISTED + extra)
             if extra:
                 chosen[it, c, place, 0, LISTED] = source[COL_BLOCKS]
@@ -190,7 +190,7 @@
                     ].reshape(2, Y, 8, SIDE)
                 return carry
 
-            lax.fori_loop(first, last, one, 0, unroll=2)
+            lax.fori_loop(first, last, one, 0, unroll=min(4, last - first))
 
         def pair_copy(c, part):
             rows = pl.ds(part * HALF, HALF)

time: 120 us -> 119 us (level)
  no operation moved by 1% of the time
where the time goes in v5:
time: 119 us; the launch traced here: 118 us
  Pallas kernels  117 us (98%)
  local copies, waits for them, and re-layouts  1.67 us (1%)
    pallas_call x1, Pallas kernels, local(): pl.pallas_call(kernel, out_shape=jax.ShapeDtypeStruct(flow_panels.shape,...  117 us

profile of v5, /device:TPU:1, one launch (start us, length us, event | category | flops | bytes accessed | tf_op | source)
XLA Modules:
  0.0 118.4 jit_solution(9270507640120931543)
XLA Ops:
  0.0 116.7 %shard_map.55 = f32[8,8192]{1,0:T(8,128)} custom-call(f32[8,8192]{1,0:T(8,128)} %flow.1, f32[192,128,128]{2,1,0:T(8,128)} %tiles.1, s32[2,192]{1,0:T(2,128)} %bitcast.3, s32[16,32]{1,0:T(8,128)} %bitcast.2, s32[2,8,64]{2,1,0:T(8,128)} %masks.1), custom_call_target="tpu_custom_call" | custom-call | tf_op jit(solution)/shard_map/pallas_call | solution.py:417
  116.8 1.7 %copy.7 = f32[8,8192]{1,0:T(8,128)} copy(f32[8,8192]{1,0:T(8,128)} %shard_map.55) | data formatting | bytes 524288
